TPU v7x, 128 devices: a whole 4x4x4 slice. The times are simulated.
128 devices in a mesh: ctx: 32 (over x, y, core), grp: 4 (over z).
Axes of the slice: x: 4, y: 4, z: 4, core: 2. Of those that a mesh axis runs over, the one named last changes fastest.
Arguments:
- query: bfloat16 [32, 2, 128, 576], P('grp', None, 'ctx'), may hold values from -40 to 40
- latent_cache: bfloat16 [32, 65536, 576], P('grp', 'ctx'), may hold values from -5.5 to 5.5
- context_lengths: int32 [32], P('grp'), may hold values from 32768 to 65534, as said below
- draft_positions: int32 [32, 2], P('grp'), may hold values from 32768 to 65535, as said below
- value_up: bfloat16 [128, 512, 128], P(('ctx', 'grp')), may hold values from -1 to 1
- out_proj: bfloat16 [16384, 7168], P(('ctx', 'grp')), may hold values from -0.046875 to 0.046875
Outputs:
- attended: bfloat16 [32, 2, 7168], P('grp', None, 'ctx')
Inputs may be any that keep to these rules, and one draw needn't show every extreme that they name: `context_lengths`: request 0 has 65534 committed positions and request 1 has 32768. `draft_positions`: draft slots of a request lie at or after its committed length and rise strictly along the drafts; request 0's last draft is at slot 65535 and request 1's first draft at its committed length.
All inputs are finite; a program needn't handle non-finite values.
Results may differ from a plain program's by a relative error of at most 0.03.
Values may be sent and summed in bfloat16 or wider, within the bound.
A program may use at most 128 MiB of HBM per device.

v0:
```python
import math

import jax
import jax.numpy as jnp
from jax import lax
from jax.sharding import PartitionSpec as P

LAT = 512
ROPE = 64
NOPE = 128


NEG_FILL = -1e30
YARN_GAIN = (0.1 * math.log(40.0) + 1.0) ** 2


def visible_mask(key_pos, lengths, positions):
    draft_count = positions.shape[-1]
    committed = key_pos[None, :] < lengths[:, None]
    matches = key_pos[None, None, :] == positions[:, :, None]
    draft_order = jnp.arange(draft_count, dtype=jnp.int32)
    earlier = draft_order[None, :] <= draft_order[:, None]
    drafts = jnp.any(earlier[None, :, :, None] & matches[:, None, :, :], axis=2)
    return committed[:, None, :] | drafts


def local(query, latent_cache, context_lengths, draft_positions, value_up, out_proj):
    score_scale = (NOPE + ROPE) ** (-0.5) * YARN_GAIN
    query_all = lax.all_gather(query, "ctx", axis=2, tiled=True)
    block_len = latent_cache.shape[1]
    key_pos = lax.axis_index("ctx") * block_len + jnp.arange(block_len, dtype=jnp.int32)
    visible = visible_mask(key_pos, context_lengths, draft_positions)[:, :, None, :]
    scores = (
        jnp.einsum("rshc,rkc->rshk", query_all, latent_cache, preferred_element_type=jnp.float32)
        * score_scale
    )
    block_max = jnp.max(jnp.where(visible, scores, NEG_FILL), axis=-1)
    weights = jnp.where(visible, jnp.exp(scores - block_max[..., None]), 0.0)
    block_total = jnp.sum(weights, axis=-1)
    rounded = weights.astype(jnp.bfloat16)
    block_numer = jnp.einsum(
        "rshk,rkc->rshc", rounded, latent_cache[:, :, :LAT], preferred_element_type=jnp.float32
    )
    global_max = lax.pmax(block_max, "ctx")
    factor = jnp.exp(block_max - global_max)
    denominator = lax.psum_scatter(block_total * factor, "ctx", scatter_dimension=2, tiled=True)
    scaled = (block_numer * factor[..., None]).astype(jnp.bfloat16)
    numerator = lax.psum_scatter(
        scaled.astype(jnp.float32).astype(jnp.bfloat16), "ctx", scatter_dimension=2, tiled=True
    ).astype(jnp.float32)
    latent_out = (numerator / denominator[..., None]).astype(jnp.bfloat16)
    owned_heads = lax.all_to_all(latent_out, "grp", split_axis=2, concat_axis=0, tiled=True)
    head_values = jnp.einsum(
        "rshc,hcv->rshv", owned_heads, value_up, preferred_element_type=jnp.float32
    ).astype(jnp.bfloat16)
    local_heads = value_up.shape[0]
    value_width = value_up.shape[2]
    flat_values = head_values.reshape(
        head_values.shape[0], head_values.shape[1], local_heads * value_width
    )
    partial_terms = jnp.einsum(
        "rsk,kd->rsd", flat_values, out_proj, preferred_element_type=jnp.float32
    )
    columns = lax.psum_scatter(
        partial_terms.astype(jnp.bfloat16), "ctx", scatter_dimension=2, tiled=True
    )
    result = lax.psum_scatter(columns, "grp", scatter_dimension=0, tiled=True).astype(jnp.float32)
    return result.astype(jnp.bfloat16)


def solution(mesh):
    return jax.shard_map(
        local,
        mesh=mesh,
        in_specs=(
            P("grp", None, "ctx", None),
            P("grp", "ctx", None),
            P("grp"),
            P("grp", None),
            P(("ctx", "grp"), None, None),
            P(("ctx", "grp"), None),
        ),
        out_specs=P("grp", None, "ctx"),
        check_vma=False,
    )
```

profile of v0, /device:TPU:1, one launch (start us, length us, event | category | flops | bytes accessed | tf_op | source)
XLA Modules:
  0.0 419.5 jit_solution(1758567061612297520)
XLA Ops:
  6.5 1.7 copy.34
  8.3 0.8 broadcast_compare_fusion
  9.1 0.1 and_reduce_fusion
  9.2 0.7 broadcast_compare_fusion.1
  10.0 47.6 %all-gather.2.cloned.1.call-done = bf16[8,2,128,576]{3,0,1,2:T(8,128)(2,1)} async-done(((bf16[8,2,4,576]{3,0,1,2:T(8,128)(2,1)}), bf16[8,2,128,576]{3,0,1,2:T(8,128)(2,1)}) %all-gather.2.cloned.1.call-update) | async-done | bytes 2359312 | tf_op jit(solution)/shard_map/all_gather | solution.py:29
  57.6 18.9 %select_reduce_fusion = (f32[8,2,128]{2,1,0:T(2,128)S(1)}, f32[8,2,128,2048]{3,2,1,0:T(8,128)}) fusion(pred[8,2,2048]{2,1,0:T(4,128)(4,1)S(1)} %copy.33, bf16[8,2048,576]{1,2,0:T(8,128)(2,1)} %param.7, bf16[8,2,128,576]{3,0,1,2:T(8,128)(2,1)} %all-gather.2.cloned.1.call-done), kind=kOutput, calls=%fused_computation.6 | convolution fusion | flops 4844419072 | bytes 38051840 | tf_op jit(solution)/shard_map/rshc,rkc->rshk/dot_general | solution.py:34
  76.5 63.3 %pmax.7 = f32[8,2,128]{2,1,0:T(2,128)S(1)} all-reduce(f32[8,2,128]{2,1,0:T(2,128)S(1)} %get-tuple-element.7), channel_id=1, replica_groups=mesh['ctx'=32,'grp'=4] {'ctx'}, use_global_device_ids=true, to_apply=%region_2.3 | all-reduce | flops 2048 | bytes 16384 | tf_op jit(solution)/shard_map/pmax | solution.py:44
  139.8 8.0 %fusion.5 = f32[8,2,128]{2,1,0:T(2,128)S(1)} fusion(f32[8,2,128,2048]{3,2,1,0:T(8,128)} %get-tuple-element.8, f32[8,2,128]{2,1,0:T(2,128)S(1)} %get-tuple-element.7, pred[8,2,2048]{2,1,0:T(4,128)(4,1)S(1)} %copy.33), kind=kLoop, calls=%fused_computation.7 | loop fusion | flops 16775168 | bytes 16826368 | tf_op jit(solution)/shard_map/reduce_sum | solution.py:39
  147.8 14.4 %multiply_convert_fusion = bf16[8,2,128,512]{3,2,1,0:T(8,128)(2,1)} fusion(bf16[8,2048,576]{1,2,0:T(8,128)(2,1)} %param.7, f32[8,2,128,2048]{3,2,1,0:T(8,128)} %get-tuple-element.8, f32[8,2,128]{2,1,0:T(2,128)S(1)} %get-tuple-element.7, pred[8,2,2048]{2,1,0:T(4,128)(4,1)S(1)} %copy.33, f32[8,2,128]{2,1,0:T(2,128)S(1)} %bitcast.47), kind=kOutput, calls=%fused_computation.14 | convolution fusion | flops 4313841664 | bytes 35700736 | tf_op jit(solution)/shard_map/rshk,rkc->rshc/dot_general | solution.py:41
  162.3 4.1 copy.37
  166.5 0.6 dynamic-slice
  167.7 0.1 copy.38
  167.8 121.5 %all-reduce = f32[8,2,128]{0,1,2:T(2,128)S(1)} all-reduce(f32[8,2,128]{0,1,2:T(2,128)S(1)} %copy.38), channel_id=3, replica_groups=mesh['ctx'=32,'grp'=4] {'ctx'}, use_global_device_ids=true, to_apply=%region_5.6.clone | all-reduce | flops 2048 | bytes 16384
  289.4 0.9 divide_convert_fusion
  290.3 8.4 %all_to_all.15 = bf16[8,2,4,512]{3,1,0,2:T(2,128)(2,1)S(1)} all-to-all(bf16[8,2,4,512]{3,1,0,2:T(2,128)(2,1)S(1)} %copy.39), channel_id=1, replica_groups=mesh['ctx'=32,'grp'=4] {'grp'}, dimensions={2} | all-to-all | bytes 131072 | tf_op jit(solution)/shard_map/all_to_all | solution.py:52
  298.8 0.5 convolution_convert_fusion
  299.3 6.0 %copy.44 = bf16[32,2,7168]{0,1,2:T(2,128)(2,1)} copy(bf16[32,2,7168]{2,0,1:T(8,128)(2,1)S(1)} %convolution_convert_fusion) | data formatting | bytes 1835008
  305.3 7.0 %reshape.68 = bf16[7168,64]{1,0:T(8,128)(2,1)} reshape(bf16[7168,2,32]{2,1,0:T(2,128)(2,1)} %bitcast.41) | data formatting | bytes 1835008
  312.4 77.7 %reduce-scatter.10.cloned.1.call-done = bf16[224,64]{1,0:T(8,128)(2,1)} async-done(((bf16[7168,64]{1,0:T(8,128)(2,1)}), bf16[224,64]{1,0:T(8,128)(2,1)}) %reduce-scatter.10.cloned.1.call-update) | async-done | bytes 28688
  390.1 0.9 reshape.69
  391.0 0.1 copy.46
  391.1 0.7 reshape.70
  391.9 19.7 %reduce-scatter.12.cloned.1.call-done = bf16[8,448]{1,0:T(8,128)(2,1)} async-done(((bf16[32,448]{1,0:T(8,128)(2,1)}), bf16[8,448]{1,0:T(8,128)(2,1)}) %reduce-scatter.12.cloned.1.call-update) | async-done | bytes 7184
  411.6 1.4 reshape.71
  (22 shorter events, 0.4 us)
Async XLA Ops:
  6.5 292.2 %copy-start = (bf16[128,7168]{1,0:T(8,128)(2,1)S(1)}, bf16[128,7168]{1,0:T(8,128)(2,1)}, u32[]{:S(2)}) copy-start(bf16[128,7168]{1,0:T(8,128)(2,1)} %param.11) | copy-start | bytes 5505028
  6.5 51.1 %all-gather.2.cloned.1.call-start = ((), (), s32[]{:S(2)}) async-start(), calls=%async_computation.4 | async-start | bytes 2703360 | tf_op jit(solution)/shard_map/all_gather | solution.py:29
  8.2 281.1 %reduce-scatter.8.cloned.1.call-start = ((), (), s32[]{:S(2)}) async-start(), calls=%async_computation.5 | async-start | bytes 2162688 | tf_op jit(solution)/shard_map/reduce_scatter | solution.py:48
  147.8 18.6 %copy-start.2 = (u32[128]{0:T(128)S(1)}, u32[128]{0:T(128)}, u32[]{:S(2)}) copy-start(u32[128]{0:T(128)} %constant.22) | copy-start | bytes 1540
  147.8 150.9 %copy-start.1 = (bf16[1,512,128]{2,1,0:T(8,128)(2,1)S(1)}, bf16[1,512,128]{2,1,0:T(8,128)(2,1)}, u32[]{:S(2)}) copy-start(bf16[1,512,128]{2,1,0:T(8,128)(2,1)} %param.10) | copy-start | bytes 393220
  166.4 223.7 %reduce-scatter.10.cloned.1.call-start = ((), (), s32[]{:S(2)}) async-start(), calls=%async_computation.6 | async-start | bytes 1892352
  312.4 99.2 %reduce-scatter.12.cloned.1.call-start = ((), (), s32[]{:S(2)}) async-start(), calls=%async_computation.7 | async-start | bytes 40960
Sparse Core Ops, SparseCore 0:
  9.6 47.9 all-gather.1
  166.5 76.0 reduce-scatter.7
  312.5 77.5 reduce-scatter.9
  392.3 19.2 reduce-scatter.11
where the time goes:
time: 422 us; the launch traced here: 420 us
  blocking collectives  193 us (46%)
  waiting for transfers between devices  145 us (34%)
  matrix products  33.8 us (8%)
  local copies, waits for them, and re-layouts  22.7 us (5%)
  between operations  13.9 us (3%)
  other arithmetic  10.6 us (3%)
    unnamed x1, blocking collectives  122 us
    unnamed x6, waiting for transfers between devices  97.5 us
    pmax x1, blocking collectives, local(): global_max = lax.pmax(block_max, 'ctx')  63.3 us
    all_gather x1, waiting for transfers between devices, local(): query_all = lax.all_gather(query, 'ctx', axis=2, tiled=True)  47.6 us
    dot_general x1, matrix products, local(): jnp.einsum('rshc,rkc->rshk', query_all, latent_cache, preferred_element_t...  18.9 us
    unnamed x14, local copies, waits for them, and re-layouts  17 us
    dot_general x1, matrix products, local(): jnp.einsum('rshk,rkc->rshc', rounded, latent_cache[:, :, :LAT], preferred...  14.4 us
  transfers between devices with their start and end apart: 4, of which 3 were waited for; matrix products, arithmetic and copies ran while one was open for 1% of the time, Pallas kernels for 0%

commit v1 on v0

v1 whole, which is shorter than its diff:
```python
import math

import jax
import jax.numpy as jnp
from jax import lax
from jax.experimental import pallas as pl
from jax.experimental.pallas import tpu as pltpu
from jax.sharding import PartitionSpec as P

LAT = 512
ROPE = 64
NOPE = 128
WIDTH = LAT + ROPE
STAT = LAT + 128

YARN_GAIN = (0.1 * math.log(40.0) + 1.0) ** 2
SCALE = (NOPE + ROPE) ** -0.5 * YARN_GAIN * math.log2(math.e)
NEG_FILL = -1e30

REQ_DEV = 8
OWN = REQ_DEV // 2
KEYS = 2048
CHIPS = 16
ROWS = 16
HALF = 8 * ROWS
COLS = 896
OUT = 224
F32 = jnp.float32
BF16 = jnp.bfloat16
MESH = pl.DeviceIdType.MESH


def dot_nn(a, b):
    return jnp.dot(a, b, preferred_element_type=F32)


def dot_nt(a, b):
    return lax.dot_general(a, b, (((1,), (1,)), ((), ())), preferred_element_type=F32)


def pack_stat(lse):
    hi = lse.astype(BF16).astype(F32)
    mid = (lse - hi).astype(BF16).astype(F32)
    low = lse - hi - mid
    shape = (lse.shape[0], 128)
    lane = lax.broadcasted_iota(jnp.int32, shape, 1)
    terms = jnp.where(lane == 0, hi, jnp.where(lane == 1, mid, jnp.where(lane == 2, low, 0.0)))
    return terms.astype(BF16)


def unpack_stat(tile):
    return jnp.sum(tile.astype(F32), axis=-1, keepdims=True)


def kernel(
    len_ref, draft_ref, q_ref, cache_ref, vup_ref, proj_ref, out_ref,
    kbuf, qf, qsib, qbuf, res, psib, mbuf, rbuf, latb, wbuf, vbuf, hvall, pbuf, fbuf,
    k_sem, qp_sem, qs_sem, qr_sem, ff_sem, ps_sem, pr_sem, ms_sem, mr_sem,
    ws_sem, wr_sem, vs_sem, vr_sem, hs_sem, hr_sem, fs_sem, fr_sem,
):
    ctx = lax.axis_index("ctx")
    z = lax.axis_index("grp")
    core = lax.rem(ctx, 2)
    chip = lax.div(ctx, 2)
    x = lax.div(chip, 4)
    y = lax.rem(chip, 4)
    sib = ctx + 1 - 2 * core
    head = core * 4 + z

    def remote(src, dst, send, recv, to_ctx, to_z=None):
        where = {"ctx": to_ctx} if to_z is None else {"ctx": to_ctx, "grp": to_z}
        return pltpu.make_async_remote_copy(
            src_ref=src, dst_ref=dst, send_sem=send, recv_sem=recv,
            device_id=where, device_id_type=MESH,
        )

    def arrived(ref, sem):
        remote(ref, ref, sem, sem, sib).wait_recv()

    def left(ref, sem):
        remote(ref, ref, sem, sem, sib).wait_send()

    plane = [(dx, dy) for dx in range(4) for dy in range(4) if dx or dy]
    column = [(dc, dz) for dz in range(4) for dc in range(2) if dc or dz]

    def cache_copy(r):
        return pltpu.make_async_copy(cache_ref.at[r], kbuf.at[r], k_sem.at[r])

    for r in range(REQ_DEV):
        both = [q_ref[r, s].astype(F32) for s in range(2)]
        qf[r] = jnp.concatenate(both, axis=0)
    theirs = pl.ds((1 - core) * OWN, OWN)
    pair_q = remote(qf.at[theirs], qsib, qp_sem.at[0], qp_sem.at[1], sib)
    pair_q.start()
    for i in range(REQ_DEV):
        cache_copy((i % 2) * OWN + i // 2).start()
    pair_q.wait_recv()
    for rr in range(OWN):
        r = core * OWN + rr
        mine, other = qf[r], qsib[rr]
        first = jnp.where(core == 0, mine, other)
        second = jnp.where(core == 0, other, mine)
        qbuf[r, chip] = jnp.concatenate([first, second], axis=0).astype(BF16)
        for dx, dy in plane:
            to = lax.rem(x + dx, 4) * 4 + lax.rem(y + dy, 4)
            remote(
                qbuf.at[r, chip], qbuf.at[r, chip], qs_sem.at[rr], qr_sem.at[r], 2 * to + core
            ).start()

    rows = pl.ds(pl.multiple_of(head * 128, 128), 128)

    def cut(cc, zz):
        return proj_ref.at[:, pl.ds(pl.multiple_of(zz * 2 * COLS + cc * COLS, 128), COLS)]

    pltpu.make_async_copy(cut(core, z), wbuf.at[rows], wr_sem).start()
    pltpu.make_async_copy(vup_ref.at[0], vbuf.at[head], vr_sem).start()
    for dc, dz in column:
        cc, zz = lax.rem(core + dc, 2), lax.rem(z + dz, 4)
        remote(vup_ref.at[0], vbuf.at[head], vs_sem, vr_sem, 2 * chip + cc, zz).start()
        remote(cut(cc, zz), wbuf.at[rows], ws_sem, wr_sem, 2 * chip + cc, zz).start()

    def forward(rr):
        r = core * OWN + rr
        arrived(qbuf.at[r, pl.ds(0, CHIPS - 1)], qr_sem.at[r])
        remote(qbuf.at[r], qbuf.at[r], ff_sem.at[0, r], ff_sem.at[1, r], sib).start()

    def attend(r):
        cache_copy(r).wait()
        first_pos = ctx * KEYS
        pos = first_pos + lax.broadcasted_iota(jnp.int32, (8, KEYS), 1)
        draft = lax.div(lax.broadcasted_iota(jnp.int32, (8, KEYS), 0), 4)
        seen = (pos < len_ref[r]) | (pos == draft_ref[r, 0])
        seen = seen | ((pos == draft_ref[r, 1]) & (draft == 1))
        bias = jnp.where(seen, 0.0, NEG_FILL)
        queries = qbuf[r].reshape(CHIPS * ROWS, WIDTH)
        scores = dot_nn(queries, kbuf[r])
        scores = (scores.reshape(32, 8, KEYS) * SCALE + bias[None]).reshape(CHIPS * ROWS, KEYS)
        top = jnp.max(scores, axis=1, keepdims=True)
        weights = jnp.exp2(scores - top)
        total = jnp.sum(weights, axis=1, keepdims=True)
        numer = dot_nt(weights.astype(BF16), kbuf[r, :LAT, :])
        numer = (numer * (1.0 / total)).astype(BF16)
        stat = pack_stat(top + jnp.log2(total))
        for h in range(2):
            res[r, h, :, :LAT] = numer[h * HALF:(h + 1) * HALF]
            res[r, h, :, LAT:] = stat[h * HALF:(h + 1) * HALF]
        remote(res.at[r, 1 - core], psib.at[r], ps_sem.at[r], pr_sem.at[r], sib).start()

    def block_to(r, i):
        to = 8 * core + lax.rem(i + chip, 8)
        owner = lax.div(r, OWN)
        rr = lax.rem(r, OWN)
        dest = 2 * to + owner
        src, dst = mbuf.at[r, lax.rem(i + chip, 8)], rbuf.at[rr, chip]
        return dest, src, dst, rr

    def merge(r):
        arrived(psib.at[r], pr_sem.at[r])
        a, b = res[r, core], psib[r]
        la, lb = unpack_stat(a[:, LAT:]), unpack_stat(b[:, LAT:])
        top = jnp.maximum(la, lb)
        wa, wb = jnp.exp2(la - top), jnp.exp2(lb - top)
        both = wa + wb
        inv = 1.0 / both
        merged = a[:, :LAT].astype(F32) * (wa * inv) + b[:, :LAT].astype(F32) * (wb * inv)
        stat = pack_stat(top + jnp.log2(both))
        mbuf[r, :, :, :LAT] = merged.astype(BF16).reshape(8, ROWS, LAT)
        mbuf[r, :, :, LAT:] = stat.reshape(8, ROWS, 128)

        def send(i, carry):
            dest, src, dst, rr = block_to(r, i)

            @pl.when(dest == ctx)
            def _():
                pltpu.make_async_copy(src, dst, mr_sem.at[rr]).start()

            @pl.when(dest != ctx)
            def _():
                remote(src, dst, ms_sem.at[r, i], mr_sem.at[rr], dest).start()

            return carry

        lax.fori_loop(0, 8, send, 0)

    forward(0)

    def step(j, carry):
        @pl.when(core == 1)
        def _():
            arrived(qbuf.at[j], ff_sem.at[1, j])

        attend(j)

        @pl.when(j > 0)
        def _():
            merge(j + OWN - 1)

        @pl.when(j < OWN - 1)
        def _():
            forward(j + 1)

        @pl.when(core == 0)
        def _():
            arrived(qbuf.at[j + OWN], ff_sem.at[1, j + OWN])

        attend(j + OWN)
        merge(j)
        return carry

    lax.fori_loop(0, OWN, step, 0)
    merge(REQ_DEV - 1)

    def finish(rr, carry):
        arrived(rbuf.at[rr], mr_sem.at[rr])
        parts = rbuf[rr]
        lse = unpack_stat(parts[:, :, LAT:])
        top = jnp.max(lse, axis=0, keepdims=True)
        w = jnp.exp2(lse - top)
        w = w * (1.0 / jnp.sum(w, axis=0, keepdims=True))
        latb[rr] = jnp.sum(parts[:, :, :LAT].astype(F32) * w, axis=0).astype(BF16)
        return carry

    lax.fori_loop(0, OWN, finish, 0)

    arrived(vbuf, vr_sem)
    latent = latb[...].reshape(OWN * ROWS, LAT)
    row = lax.broadcasted_iota(jnp.int32, (16, OWN * ROWS), 1)
    at = lax.broadcasted_iota(jnp.int32, (16, OWN * ROWS), 0)
    place = (core * OWN + row // 16) * 2 + (row // 4) % 2
    row_head = ((row // 8) % 2) * 4 + row % 4
    own_slot = z * 2 + core
    for h in range(8):
        values = dot_nn(latent, vbuf[h]).astype(BF16)
        pick = jnp.where((place == at) & (row_head == h), 1.0, 0.0).astype(BF16)
        hvall[own_slot, :, h * 128:(h + 1) * 128] = dot_nn(pick, values).astype(BF16)
    for dc, dz in column:
        cc, zz = lax.rem(core + dc, 2), lax.rem(z + dz, 4)
        remote(
            hvall.at[own_slot], hvall.at[own_slot], hs_sem, hr_sem, 2 * chip + cc, zz
        ).start()
    arrived(wbuf, wr_sem)
    arrived(hvall.at[pl.ds(0, 7)], hr_sem)

    acts = jnp.concatenate(
        [(hvall[2 * g].astype(F32) + hvall[2 * g + 1].astype(F32)).astype(BF16) for g in range(4)],
        axis=0,
    )
    partial = dot_nn(acts, wbuf[...])
    for jj in range(4):
        piece = partial[:, jj * OUT:(jj + 1) * OUT]
        piece = jnp.concatenate([piece, jnp.zeros((64, 256 - OUT), F32)], axis=1)
        pbuf[jj] = piece.astype(BF16).reshape(4, 16, 256)

    def out_to(jj, dz):
        zz = lax.rem(z + dz, 4)
        dest = z * 8 + core * 4 + jj
        return dest, zz, (dest == ctx) & (zz == z)

    for dz in range(4):
        for jj in range(4):
            dest, zz, here = out_to(jj, dz)

            @pl.when(here)
            def _():
                pltpu.make_async_copy(pbuf.at[jj, zz], fbuf.at[chip], fr_sem).start()

            @pl.when(jnp.logical_not(here))
            def _():
                remote(
                    pbuf.at[jj, zz], fbuf.at[chip], fs_sem.at[jj, dz], fr_sem, dest, zz
                ).start()

    arrived(fbuf, fr_sem)
    out_ref[...] = jnp.sum(fbuf[...].astype(F32), axis=0)[:, :OUT].astype(BF16)

    pair_q.wait_send()
    for rr in range(OWN):
        r = core * OWN + rr
        left(qbuf.at[r, pl.ds(0, CHIPS - 1)], qs_sem.at[rr])
        left(qbuf.at[r], ff_sem.at[0, r])
    left(vbuf.at[pl.ds(0, 7)], vs_sem)
    left(wbuf.at[pl.ds(0, 7 * 128)], ws_sem)
    left(hvall.at[pl.ds(0, 7)], hs_sem)

    def gone(r, carry):
        left(psib.at[r], ps_sem.at[r])

        def one(i, inner):
            dest, src, dst, rr = block_to(r, i)

            @pl.when(dest != ctx)
            def _():
                left(src, ms_sem.at[r, i])

            return inner

        return lax.fori_loop(0, 8, one, carry)

    lax.fori_loop(0, REQ_DEV, gone, 0)
    for dz in range(4):
        for jj in range(4):
            dest, zz, here = out_to(jj, dz)

            @pl.when(jnp.logical_not(here))
            def _():
                left(pbuf.at[jj, zz], fs_sem.at[jj, dz])


def local(query, latent_cache, context_lengths, draft_positions, value_up, out_proj):
    dma = pltpu.SemaphoreType.DMA
    vmem = pltpu.VMEM
    flat = pl.pallas_call(
        kernel,
        out_shape=jax.ShapeDtypeStruct((16, OUT), BF16),
        in_specs=[
            pl.BlockSpec(memory_space=pltpu.SMEM),
            pl.BlockSpec(memory_space=pltpu.SMEM),
            pl.BlockSpec(memory_space=pltpu.VMEM),
            pl.BlockSpec(memory_space=pl.ANY),
            pl.BlockSpec(memory_space=pl.ANY),
            pl.BlockSpec(memory_space=pl.ANY),
        ],
        out_specs=pl.BlockSpec(memory_space=pltpu.VMEM),
        scratch_shapes=[
            vmem((REQ_DEV, WIDTH, KEYS), BF16),
            vmem((REQ_DEV, 8, WIDTH), F32),
            vmem((OWN, 8, WIDTH), F32),
            vmem((REQ_DEV, CHIPS, ROWS, WIDTH), BF16),
            vmem((REQ_DEV, 2, HALF, STAT), BF16),
            vmem((REQ_DEV, HALF, STAT), BF16),
            vmem((REQ_DEV, 8, ROWS, STAT), BF16),
            vmem((OWN, CHIPS, ROWS, STAT), BF16),
            vmem((OWN, ROWS, LAT), BF16),
            vmem((8 * 128, COLS), BF16),
            vmem((8, LAT, 128), BF16),
            vmem((8, 16, 8 * 128), BF16),
            vmem((4, 4, 16, 256), BF16),
            vmem((CHIPS, 16, 256), BF16),
            dma((REQ_DEV,)), dma((2,)), dma((OWN,)), dma((REQ_DEV,)), dma((2, REQ_DEV)),
            dma((REQ_DEV,)), dma((REQ_DEV,)), dma((REQ_DEV, 8)), dma((OWN,)),
            dma, dma, dma, dma, dma, dma, dma((4, 4)), dma,
        ],
        compiler_params=pltpu.CompilerParams(
            has_side_effects=True, vmem_limit_bytes=56 * 2**20
        ),
        name="latent_decode",
    )(context_lengths, draft_positions, query, jnp.swapaxes(latent_cache, 1, 2), value_up, out_proj)
    return flat.reshape(REQ_DEV, 2, OUT)


def solution(mesh):
    return jax.shard_map(
        local,
        mesh=mesh,
        in_specs=(
            P("grp", None, "ctx", None),
            P("grp", "ctx", None),
            P("grp"),
            P("grp", None),
            P(("ctx", "grp"), None, None),
            P(("ctx", "grp"), None),
        ),
        out_specs=P("grp", None, "ctx"),
        check_vma=False,
    )
```

time: 422 us -> 71.7 us (0.17)
  blocking collectives: 193 us -> 0 us
  waiting for transfers between devices: 145 us -> 0 us
  Pallas kernels: 0 us -> 68.9 us
  matrix products: 33.8 us -> 0 us
  local copies, waits for them, and re-layouts: 22.7 us -> 2.65 us
  between operations: 13.9 us -> 0.01 us
  other arithmetic: 10.6 us -> 0 us
    unnamed x1 -> x0, blocking collectives: 122 us -> none
    unnamed x6 -> x0, waiting for transfers between devices: 97.5 us -> none
    pallas_call x0 -> x1, Pallas kernels: none -> 68.9 us  [local(): pl.pallas_call(kernel, out_shape=jax.ShapeDtypeStruct((16, OUT), BF16), i...]
    pmax x1 -> x0, blocking collectives: 63.3 us -> none  [local(): global_max = lax.pmax(block_max, 'ctx')]
    all_gather x1 -> x0, waiting for transfers between devices: 47.6 us -> none  [local(): query_all = lax.all_gather(query, 'ctx', axis=2, tiled=True)]
    dot_general x3 -> x0, matrix products: 33.8 us -> none  [the longest x1 18.9 us: local(): jnp.einsum('rshc,rkc->rshk', query_all, latent_cache, preferred_element_t...]
    unnamed x14 -> x1, local copies, waits for them, and re-layouts: 17 us -> 1.34 us
    all_to_all x1 -> x0, blocking collectives: 8.4 us -> none  [local(): lax.all_to_all(latent_out, 'grp', split_axis=2, concat_axis=0, tiled=True)]
  transfers between devices with their start and end apart: 4 -> 0, of which waited for: 3 -> 0; matrix products, arithmetic and copies ran while one was open for 1% -> 0% of each run, Pallas kernels for 0% -> 0%
where the time goes in v1:
time: 71.7 us; the launch traced here: 71.5 us
  Pallas kernels  68.9 us (96%)
  local copies, waits for them, and re-layouts  2.65 us (4%)
    pallas_call x1, Pallas kernels, local(): pl.pallas_call(kernel, out_shape=jax.ShapeDtypeStruct((16, OUT), BF16), i...  68.9 us

profile of v1, /device:TPU:1, one launch (start us, length us, event | category | flops | bytes accessed | tf_op | source)
XLA Modules:
  0.0 71.5 jit_solution(1632311564986345008)
XLA Ops:
  0.0 1.3 %copy.7.draft_ref = s32[8,2]{1,0:T(8,128)} copy(s32[8,2]{0,1:T(2,128)} %param.9) | data formatting | bytes 128 | tf_op args[3]
  1.3 68.9 %latent_decode.1 = bf16[16,224]{1,0:T(8,128)(2,1)} custom-call(s32[8]{0:T(128)} %len_ref.1, s32[8,2]{1,0:T(8,128)} %copy.7.draft_ref, bf16[8,2,4,576]{3,2,1,0:T(4,128)(2,1)} %q_ref.1, bf16[8,576,2048]{2,1,0:T(8,128)(2,1)} %bitcast.1, bf16[1,512,128]{2,1,0:T(8,128)(2,1)} %vup_ref.1, bf16[128,7168]{1,0:T(8,128)(2,1)} %proj_ref.1), custom_call_target="tpu_custom_call" | custom-call | tf_op jit(solution)/shard_map/latent_decode/pallas_call | solution.py:312
  70.2 1.3 %reshape.3 = bf16[8,2,224]{2,1,0:T(2,128)(2,1)} reshape(bf16[16,224]{1,0:T(8,128)(2,1)} %latent_decode.1) | data formatting | bytes 14336 | tf_op jit(solution)/shard_map/reshape | solution.py:348

commit v2 on v1

v2 whole, which is shorter than its diff:
```python
import math

import jax
import jax.numpy as jnp
from jax import lax
from jax.experimental import pallas as pl
from jax.experimental.pallas import tpu as pltpu
from jax.sharding import PartitionSpec as P

LAT = 512
ROPE = 64
NOPE = 128
WIDTH = LAT + ROPE
STAT = LAT + 128

YARN_GAIN = (0.1 * math.log(40.0) + 1.0) ** 2
SCALE = (NOPE + ROPE) ** -0.5 * YARN_GAIN * math.log2(math.e)
NEG_FILL = -1e30

REQ_DEV = 8
OWN = REQ_DEV // 2
KEYS = 2048
CHIPS = 16
ROWS = 16
HALF = 8 * ROWS
COLS = 896
OUT = 224
F32 = jnp.float32
BF16 = jnp.bfloat16
MESH = pl.DeviceIdType.MESH


def dot_nn(a, b):
    return jnp.dot(a, b, preferred_element_type=F32)


def dot_nt(a, b):
    return lax.dot_general(a, b, (((1,), (1,)), ((), ())), preferred_element_type=F32)


def pack_stat(lse):
    hi = lse.astype(BF16).astype(F32)
    mid = (lse - hi).astype(BF16).astype(F32)
    low = lse - hi - mid
    shape = (lse.shape[0], 128)
    lane = lax.broadcasted_iota(jnp.int32, shape, 1)
    terms = jnp.where(lane == 0, hi, jnp.where(lane == 1, mid, jnp.where(lane == 2, low, 0.0)))
    return terms.astype(BF16)


def unpack_stat(tile):
    return jnp.sum(tile.astype(F32), axis=-1, keepdims=True)


def kernel(
    len_ref, draft_ref, q_ref, cache_ref, vup_ref, proj_ref, out_ref,
    kbuf, qf, qsib, qbuf, res, psib, mbuf, ubuf, vout, rbuf, lbuf, latb, wbuf, vbuf, hvall, pbuf, fbuf,
    k_sem, qp_sem, q1s_sem, q1r_sem, q2s_sem, q2r_sem, ff_sem, ps_sem, pr_sem,
    us_sem, ur_sem, ns_sem, nr_sem, ls_sem, lr_sem, ws_sem, wr_sem, vs_sem, vr_sem, hs_sem, hr_sem, fs_sem, fr_sem,
):
    ctx = lax.axis_index("ctx")
    z = lax.axis_index("grp")
    core = lax.rem(ctx, 2)
    chip = lax.div(ctx, 2)
    x = lax.div(chip, 4)
    y = lax.rem(chip, 4)
    sib = ctx + 1 - 2 * core
    head = core * 4 + z

    def remote(src, dst, send, recv, to_ctx, to_z=None):
        where = {"ctx": to_ctx} if to_z is None else {"ctx": to_ctx, "grp": to_z}
        return pltpu.make_async_remote_copy(
            src_ref=src, dst_ref=dst, send_sem=send, recv_sem=recv,
            device_id=where, device_id_type=MESH,
        )

    def arrived(ref, sem):
        remote(ref, ref, sem, sem, sib).wait_recv()

    def left(ref, sem):
        remote(ref, ref, sem, sem, sib).wait_send()

    def turned(rr):
        odd = lax.rem(rr, 2)
        return x + odd * (y - x), y + odd * (x - y), odd

    def chip_at(u, v, odd):
        return (u * 4 + v) + odd * 3 * (v - u)

    column = [(dc, dz) for dz in range(4) for dc in range(2) if dc or dz]

    def cache_copy(r):
        return pltpu.make_async_copy(cache_ref.at[r], kbuf.at[r], k_sem.at[r])

    gate = pltpu.get_barrier_semaphore()
    plane = [(dx, dy) for dx in range(4) for dy in range(4) if dx or dy]
    near = [(sib, z)]
    for d in range(1, 4):
        for dc in range(2):
            near.append((2 * chip + lax.rem(core + dc, 2), lax.rem(z + d, 4)))
    for dx, dy in plane:
        near.append((2 * (lax.rem(x + dx, 4) * 4 + lax.rem(y + dy, 4)) + core, z))
    for to_ctx, to_z in near:
        pl.semaphore_signal(
            gate, inc=1, device_id={"ctx": to_ctx, "grp": to_z}, device_id_type=MESH
        )
    for i in range(REQ_DEV):
        cache_copy((i % 2) * OWN + i // 2).start()

    for r in range(REQ_DEV):
        both = [q_ref[r, s].astype(F32) for s in range(2)]
        qf[r] = jnp.concatenate(both, axis=0)
    pl.semaphore_wait(gate, len(near))
    theirs = pl.ds((1 - core) * OWN, OWN)
    pair_q = remote(qf.at[theirs], qsib, qp_sem.at[0], qp_sem.at[1], sib)
    pair_q.start()
    pair_q.wait_recv()
    for rr in range(OWN):
        r = core * OWN + rr
        mine, other = qf[r], qsib[rr]
        first = jnp.where(core == 0, mine, other)
        second = jnp.where(core == 0, other, mine)
        u, v, odd = turned(rr)
        slot = u * 4 + v
        qbuf[r, slot] = jnp.concatenate([first, second], axis=0).astype(BF16)
        if rr == 0:
            for dx, dy in plane:
                to = lax.rem(x + dx, 4) * 4 + lax.rem(y + dy, 4)
                remote(
                    qbuf.at[r, slot], qbuf.at[r, slot], q2s_sem.at[rr], q2r_sem.at[rr],
                    2 * to + core,
                ).start()
            continue
        for d in range(1, 4):
            to = chip_at(u, lax.rem(v + d, 4), odd)
            remote(
                qbuf.at[r, slot], qbuf.at[r, slot], q1s_sem.at[rr], q1r_sem.at[rr], 2 * to + core
            ).start()

    rows = pl.ds(pl.multiple_of(head * 128, 128), 128)

    def column_group(cc, zz):
        return lax.rem(x + 4 + zz - 2 * zz * cc, 4) * 2 + lax.rem(cc + y, 2)

    def cut(cc, zz):
        return proj_ref.at[:, pl.ds(pl.multiple_of(column_group(cc, zz) * COLS, 128), COLS)]

    pltpu.make_async_copy(cut(core, z), wbuf.at[rows], wr_sem).start()
    pltpu.make_async_copy(vup_ref.at[0], vbuf.at[head], vr_sem).start()
    for dc, dz in column:
        cc, zz = lax.rem(core + dc, 2), lax.rem(z + dz, 4)
        remote(vup_ref.at[0], vbuf.at[head], vs_sem, vr_sem, 2 * chip + cc, zz).start()
        remote(cut(cc, zz), wbuf.at[rows], ws_sem, wr_sem, 2 * chip + cc, zz).start()

    def spread(rr):
        r = core * OWN + rr
        u, v, odd = turned(rr)
        arrived(qbuf.at[r, pl.ds(0, 3)], q1r_sem.at[rr])
        line = qbuf.at[r, pl.ds(4 * u, 4)]
        for d in range(1, 4):
            to = chip_at(lax.rem(u + d, 4), v, odd)
            remote(line, line, q2s_sem.at[rr], q2r_sem.at[rr], 2 * to + core).start()

    def forward(rr, count):
        r = core * OWN + rr
        arrived(qbuf.at[r, pl.ds(0, count)], q2r_sem.at[rr])
        remote(qbuf.at[r], qbuf.at[r], ff_sem.at[0, r], ff_sem.at[1, r], sib).start()

    def attend(r):
        cache_copy(r).wait()
        first_pos = ctx * KEYS
        pos = first_pos + lax.broadcasted_iota(jnp.int32, (8, KEYS), 1)
        draft = lax.div(lax.broadcasted_iota(jnp.int32, (8, KEYS), 0), 4)
        seen = (pos < len_ref[r]) | (pos == draft_ref[0, r])
        seen = seen | ((pos == draft_ref[1, r]) & (draft == 1))
        bias = jnp.where(seen, 0.0, NEG_FILL)
        queries = qbuf[r].reshape(CHIPS * ROWS, WIDTH)
        scores = dot_nn(queries, kbuf[r])
        scores = (scores.reshape(32, 8, KEYS) * SCALE + bias[None]).reshape(CHIPS * ROWS, KEYS)
        top = jnp.max(scores, axis=1, keepdims=True)
        weights = jnp.exp2(scores - top)
        total = jnp.sum(weights, axis=1, keepdims=True)
        numer = dot_nt(weights.astype(BF16), kbuf[r, :LAT, :])
        numer = (numer * (1.0 / total)).astype(BF16)
        stat = pack_stat(top + jnp.log2(total))
        for h in range(2):
            res[r, h, :, :LAT] = numer[h * HALF:(h + 1) * HALF]
            res[r, h, :, LAT:] = stat[h * HALF:(h + 1) * HALF]
        remote(res.at[r, 1 - core], psib.at[r], ps_sem.at[r], pr_sem.at[r], sib).start()

    def line_to(r, i):
        owner, rr = lax.div(r, OWN), lax.rem(r, OWN)
        u, v, odd = turned(rr)
        dest = 2 * chip_at(2 * core + i, v, odd) + owner
        return dest, mbuf.at[r, i], ubuf.at[rr, u], rr

    def merge(r):
        arrived(psib.at[r], pr_sem.at[r])
        a, b = res[r, core], psib[r]
        la, lb = unpack_stat(a[:, LAT:]), unpack_stat(b[:, LAT:])
        top = jnp.maximum(la, lb)
        wa, wb = jnp.exp2(la - top), jnp.exp2(lb - top)
        both = wa + wb
        inv = 1.0 / both
        merged = a[:, :LAT].astype(F32) * (wa * inv) + b[:, :LAT].astype(F32) * (wb * inv)
        stat = pack_stat(top + jnp.log2(both))
        mbuf[r, :, :, :, :LAT] = merged.astype(BF16).reshape(2, 4, ROWS, LAT)
        mbuf[r, :, :, :, LAT:] = stat.reshape(2, 4, ROWS, 128)

    def send_line(r):
        for i in range(2):
            dest, src, dst, rr = line_to(r, i)

            @pl.when(dest == ctx)
            def _():
                pltpu.make_async_copy(src, dst, ur_sem.at[rr]).start()

            @pl.when(dest != ctx)
            def _():
                remote(src, dst, us_sem.at[r, i], ur_sem.at[rr], dest).start()

    def block_to(r, i):
        owner = lax.div(r, OWN)
        u, v, odd = turned(OWN - 1)
        t = lax.rem(i + 2 * v + u, 8)
        to_u, to_v = 2 * core + lax.div(t, 4), lax.rem(t, 4)
        dest = 2 * chip_at(to_u, to_v, odd) + owner
        return dest, mbuf.at[r, lax.div(t, 4), to_v], lbuf.at[chip]

    def send_blocks(r):
        def one(i, carry):
            dest, src, dst = block_to(r, i)

            @pl.when(dest == ctx)
            def _():
                pltpu.make_async_copy(src, dst, lr_sem).start()

            @pl.when(dest != ctx)
            def _():
                remote(src, dst, ls_sem.at[lax.div(r, OWN), i], lr_sem, dest).start()

            return carry

        lax.fori_loop(0, 8, one, 0)

    def joined(parts):
        lse = unpack_stat(parts[:, :, LAT:])
        top = jnp.max(lse, axis=0, keepdims=True)
        w = jnp.exp2(lse - top)
        total = jnp.sum(w, axis=0, keepdims=True)
        w = w * (1.0 / total)
        latent = jnp.sum(parts[:, :, :LAT].astype(F32) * w, axis=0)
        return latent, (top + jnp.log2(total))[0]

    def fold(rr):
        u, v, odd = turned(rr)
        arrived(ubuf.at[rr], ur_sem.at[rr])
        latent, lse = joined(ubuf[rr].reshape(4, 4 * ROWS, STAT))
        vout[rr, :, :, :LAT] = latent.astype(BF16).reshape(4, ROWS, LAT)
        vout[rr, :, :, LAT:] = pack_stat(lse).reshape(4, ROWS, 128)
        rbuf[rr, v] = vout[rr, v]
        for d in range(1, 4):
            to_v = lax.rem(v + d, 4)
            dest = 2 * chip_at(u, to_v, odd) + core
            remote(vout.at[rr, to_v], rbuf.at[rr, v], ns_sem.at[rr], nr_sem.at[rr], dest).start()

    for rr in range(1, OWN):
        spread(rr)
    forward(0, CHIPS - 1)

    def step(j, carry):
        @pl.when(core == 1)
        def _():
            arrived(qbuf.at[j], ff_sem.at[1, j])

        attend(j)

        @pl.when(j > 0)
        def _():
            merge(j + OWN - 1)
            send_line(j + OWN - 1)

        @pl.when(j < OWN - 1)
        def _():
            forward(j + 1, 12)

        @pl.when(core == 0)
        def _():
            arrived(qbuf.at[j + OWN], ff_sem.at[1, j + OWN])

        attend(j + OWN)
        merge(j)

        @pl.when(j < OWN - 1)
        def _():
            send_line(j)

        @pl.when(j == OWN - 1)
        def _():
            send_blocks(j)

        @pl.when(j >= 2)
        def _():
            fold(j - 2)

        return carry

    lax.fori_loop(0, OWN, step, 0)
    merge(REQ_DEV - 1)
    send_blocks(REQ_DEV - 1)
    fold(OWN - 2)

    def finish(rr, carry):
        arrived(rbuf.at[rr, pl.ds(0, 3)], nr_sem.at[rr])
        latent, lse = joined(rbuf[rr])
        latb[rr] = latent.astype(BF16)
        return carry

    lax.fori_loop(0, OWN - 1, finish, 0)
    arrived(lbuf, lr_sem)
    latb[OWN - 1] = joined(lbuf[...])[0].astype(BF16)

    arrived(vbuf, vr_sem)
    latent = latb[...].reshape(OWN * ROWS, LAT)
    row = lax.broadcasted_iota(jnp.int32, (16, OWN * ROWS), 1)
    at = lax.broadcasted_iota(jnp.int32, (16, OWN * ROWS), 0)
    place = ((row // 8) % 2) * 8 + (row // 16) * 2 + (row // 4) % 2
    own_slot = z * 2 + core
    for hz in range(4):
        found = jnp.zeros((16, 128), F32)
        for cc in range(2):
            values = dot_nn(latent, vbuf[cc * 4 + hz]).astype(BF16)
            keep = (place == at) & (row % 4 == hz) & ((row // 8) % 2 == cc)
            found += dot_nn(jnp.where(keep, 1.0, 0.0).astype(BF16), values)
        hvall[own_slot, :, hz * 128:(hz + 1) * 128] = found.astype(BF16)
    for dc, dz in column:
        cc, zz = lax.rem(core + dc, 2), lax.rem(z + dz, 4)
        remote(
            hvall.at[own_slot], hvall.at[own_slot], hs_sem, hr_sem, 2 * chip + cc, zz
        ).start()
    arrived(wbuf, wr_sem)
    arrived(hvall.at[pl.ds(0, 7)], hr_sem)

    def group_acts(g):
        a, b = hvall[2 * g].astype(F32), hvall[2 * g + 1].astype(F32)
        left = jnp.concatenate([a[:8], b[:8]], axis=0)
        right = jnp.concatenate([a[8:], b[8:]], axis=0)
        return jnp.concatenate([left, right], axis=1)

    acts = jnp.concatenate([group_acts(g) for g in range(4)], axis=0).astype(BF16)
    partial = dot_nn(acts, wbuf[...])
    for jj in range(4):
        piece = partial[:, jj * OUT:(jj + 1) * OUT]
        piece = jnp.concatenate([piece, jnp.zeros((64, 256 - OUT), F32)], axis=1)
        pbuf[jj] = piece.astype(BF16).reshape(4, 16, 256)

    def out_to(jj, dz):
        zz = lax.rem(z + dz, 4)
        dest = column_group(core, z) * 4 + jj
        return dest, zz, (dest == ctx) & (zz == z)

    for dz in range(4):
        for jj in range(4):
            dest, zz, here = out_to(jj, dz)

            @pl.when(here)
            def _():
                pltpu.make_async_copy(pbuf.at[jj, zz], fbuf.at[chip], fr_sem).start()

            @pl.when(jnp.logical_not(here))
            def _():
                remote(
                    pbuf.at[jj, zz], fbuf.at[chip], fs_sem.at[jj, dz], fr_sem, dest, zz
                ).start()

    arrived(fbuf, fr_sem)
    result = jnp.sum(fbuf[...].astype(F32), axis=0)[:, :OUT]
    for r in range(REQ_DEV):
        out_ref[r] = result[2 * r:2 * r + 2].astype(BF16)

    pair_q.wait_send()
    for rr in range(OWN):
        r = core * OWN + rr
        left(qbuf.at[r], ff_sem.at[0, r])
        if rr == 0:
            left(qbuf.at[r, pl.ds(0, CHIPS - 1)], q2s_sem.at[rr])
        else:
            left(qbuf.at[r, pl.ds(0, 3)], q1s_sem.at[rr])
            left(qbuf.at[r, pl.ds(0, 12)], q2s_sem.at[rr])
        if rr < OWN - 1:
            left(rbuf.at[rr, pl.ds(0, 3)], ns_sem.at[rr])
    left(vbuf.at[pl.ds(0, 7)], vs_sem)
    left(wbuf.at[pl.ds(0, 7 * 128)], ws_sem)
    left(hvall.at[pl.ds(0, 7)], hs_sem)

    def gone(r, carry):
        left(psib.at[r], ps_sem.at[r])

        @pl.when(lax.rem(r, OWN) < OWN - 1)
        def _():
            for i in range(2):
                dest, src, dst, rr = line_to(r, i)

                @pl.when(dest != ctx)
                def _():
                    left(src, us_sem.at[r, i])

        @pl.when(lax.rem(r, OWN) == OWN - 1)
        def _():
            for i in range(8):
                dest, src, dst = block_to(r, i)

                @pl.when(dest != ctx)
                def _():
                    left(src, ls_sem.at[lax.div(r, OWN), i])

        return carry

    lax.fori_loop(0, REQ_DEV, gone, 0)
    for dz in range(4):
        for jj in range(4):
            dest, zz, here = out_to(jj, dz)

            @pl.when(jnp.logical_not(here))
            def _():
                left(pbuf.at[jj, zz], fs_sem.at[jj, dz])


def local(query, latent_cache, context_lengths, draft_positions, value_up, out_proj):
    dma = pltpu.SemaphoreType.DMA
    vmem = pltpu.VMEM
    return pl.pallas_call(
        kernel,
        out_shape=jax.ShapeDtypeStruct((REQ_DEV, 2, OUT), BF16),
        in_specs=[
            pl.BlockSpec(memory_space=pltpu.SMEM),
            pl.BlockSpec(memory_space=pltpu.SMEM),
            pl.BlockSpec(memory_space=pltpu.VMEM),
            pl.BlockSpec(memory_space=pl.ANY),
            pl.BlockSpec(memory_space=pl.ANY),
            pl.BlockSpec(memory_space=pl.ANY),
        ],
        out_specs=pl.BlockSpec(memory_space=pltpu.VMEM),
        scratch_shapes=[
            vmem((REQ_DEV, WIDTH, KEYS), BF16),
            vmem((REQ_DEV, 8, WIDTH), F32),
            vmem((OWN, 8, WIDTH), F32),
            vmem((REQ_DEV, CHIPS, ROWS, WIDTH), BF16),
            vmem((REQ_DEV, 2, HALF, STAT), BF16),
            vmem((REQ_DEV, HALF, STAT), BF16),
            vmem((REQ_DEV, 2, 4, ROWS, STAT), BF16),
            vmem((OWN, 4, 4, ROWS, STAT), BF16),
            vmem((OWN, 4, ROWS, STAT), BF16),
            vmem((OWN, 4, ROWS, STAT), BF16),
            vmem((CHIPS, ROWS, STAT), BF16),
            vmem((OWN, ROWS, LAT), BF16),
            vmem((8 * 128, COLS), BF16),
            vmem((8, LAT, 128), BF16),
            vmem((8, 16, 4 * 128), BF16),
            vmem((4, 4, 16, 256), BF16),
            vmem((CHIPS, 16, 256), BF16),
            dma((REQ_DEV,)), dma((2,)), dma((OWN,)), dma((OWN,)), dma((OWN,)), dma((OWN,)),
            dma((2, REQ_DEV)), dma((REQ_DEV,)), dma((REQ_DEV,)),
            dma((REQ_DEV, 2)), dma((OWN,)), dma((OWN,)), dma((OWN,)), dma((2, 8)), dma,
            dma, dma, dma, dma, dma, dma, dma((4, 4)), dma,
        ],
        compiler_params=pltpu.CompilerParams(
            collective_id=0, has_side_effects=True, vmem_limit_bytes=56 * 2**20
        ),
        name="latent_decode",
    )(
        context_lengths, jnp.swapaxes(draft_positions, 0, 1), query,
        jnp.swapaxes(latent_cache, 1, 2), value_up, out_proj,
    )


def solution(mesh):
    return jax.shard_map(
        local,
        mesh=mesh,
        in_specs=(
            P("grp", None, "ctx", None),
            P("grp", "ctx", None),
            P("grp"),
            P("grp", None),
            P(("ctx", "grp"), None, None),
            P(("ctx", "grp"), None),
        ),
        out_specs=P("grp", None, "ctx"),
        check_vma=False,
    )
```

time: 71.7 us -> 62.6 us (0.87)
  Pallas kernels: 68.9 us -> 61.1 us
  local copies, waits for them, and re-layouts: 2.65 us -> 1.3 us
    pallas_call x1, Pallas kernels: 68.9 us -> 61.1 us  [local(): pl.pallas_call(kernel, out_shape=jax.ShapeDtypeStruct((REQ_DEV, 2, OUT),...]
    reshape x1 -> x0, local copies, waits for them, and re-layouts: 1.31 us -> none  [local(): return flat.reshape(REQ_DEV, 2, OUT)]
where the time goes in v2:
time: 62.6 us; the launch traced here: 62.4 us
  Pallas kernels  61.1 us (98%)
  local copies, waits for them, and re-layouts  1.3 us (2%)
    pallas_call x1, Pallas kernels, local(): pl.pallas_call(kernel, out_shape=jax.ShapeDtypeStruct((REQ_DEV, 2, OUT),...  61.1 us
    unnamed x1, local copies, waits for them, and re-layouts  1.3 us

profile of v2, /device:TPU:1, one launch (start us, length us, event | category | flops | bytes accessed | tf_op | source)
XLA Modules:
  0.0 62.4 jit_solution(7230479657492631415)
XLA Ops:
  0.0 61.1 %latent_decode.1 = bf16[8,2,224]{2,1,0:T(2,128)(2,1)} custom-call(s32[8]{0:T(128)} %len_ref.1, s32[2,8]{1,0:T(2,128)} %bitcast.3, bf16[8,2,4,576]{3,2,1,0:T(4,128)(2,1)} %q_ref.1, bf16[8,576,2048]{2,1,0:T(8,128)(2,1)} %bitcast.2, bf16[1,512,128]{2,1,0:T(8,128)(2,1)} %vup_ref.1, bf16[128,7168]{1,0:T(8,128)(2,1)} %proj_ref.1), custom_call_target="tpu_custom_call" | custom-call | tf_op jit(solution)/shard_map/latent_decode/pallas_call | solution.py:432
  61.1 1.3 %copy.8 = bf16[8,2,224]{2,1,0:T(2,128)(2,1)} copy(bf16[8,2,224]{2,1,0:T(2,128)(2,1)} %latent_decode.1) | data formatting | bytes 14336

commit v3 on v2

v3 whole, which is shorter than its diff:
```python
import math

import jax
import jax.numpy as jnp
from jax import lax
from jax.experimental import pallas as pl
from jax.experimental.pallas import tpu as pltpu
from jax.sharding import PartitionSpec as P

LAT = 512
ROPE = 64
NOPE = 128
WIDTH = LAT + ROPE
PADDED = 640
PATHS = (slice(0, 256), slice(256, PADDED))
STAT = LAT + 128

YARN_GAIN = (0.1 * math.log(40.0) + 1.0) ** 2
SCALE = (NOPE + ROPE) ** -0.5 * YARN_GAIN * math.log2(math.e)
NEG_FILL = -1e30

REQ_DEV = 8
OWN = REQ_DEV // 2
KEYS = 2048
CHIPS = 16
ROWS = 16
HALF = 8 * ROWS
COLS = 896
OUT = 224
PART = 512
F32 = jnp.float32
BF16 = jnp.bfloat16
MESH = pl.DeviceIdType.MESH


def dot_nn(a, b):
    return jnp.dot(a, b, preferred_element_type=F32)


def dot_nt(a, b):
    return lax.dot_general(a, b, (((1,), (1,)), ((), ())), preferred_element_type=F32)


def pack_stat(lse):
    hi = lse.astype(BF16).astype(F32)
    mid = (lse - hi).astype(BF16).astype(F32)
    low = lse - hi - mid
    shape = (lse.shape[0], 128)
    lane = lax.broadcasted_iota(jnp.int32, shape, 1)
    terms = jnp.where(lane == 0, hi, jnp.where(lane == 1, mid, jnp.where(lane == 2, low, 0.0)))
    return terms.astype(BF16)


def unpack_stat(tile):
    return jnp.sum(tile.astype(F32), axis=-1, keepdims=True)


def kernel(
    len_ref, draft_ref, q_ref, cache_ref, vup_ref, proj_ref, out_ref,
    kbuf, store_a, store_b, qf, qsib, qbuf, res, psib, mbuf, ubuf, vout, rbuf, lbuf, latb, wbuf, vbuf, hvall, sort, pbuf, fbuf,
    k_sem, qp_sem, q1s_sem, q1r_sem, q2s_sem, q2r_sem, ff_sem, ps_sem, pr_sem,
    us_sem, ur_sem, ns_sem, nr_sem, ls_sem, lr_sem, ws_sem, wr_sem, vs_sem, vr_sem, vf_sem, hs_sem, hr_sem, fs_sem, fr_sem,
):
    ctx = lax.axis_index("ctx")
    z = lax.axis_index("grp")
    core = lax.rem(ctx, 2)
    chip = lax.div(ctx, 2)
    x = lax.div(chip, 4)
    y = lax.rem(chip, 4)
    sib = ctx + 1 - 2 * core
    head = core * 4 + z

    def remote(src, dst, send, recv, to_ctx, to_z=None):
        where = {"ctx": to_ctx} if to_z is None else {"ctx": to_ctx, "grp": to_z}
        return pltpu.make_async_remote_copy(
            src_ref=src, dst_ref=dst, send_sem=send, recv_sem=recv,
            device_id=where, device_id_type=MESH,
        )

    def arrived(ref, sem):
        remote(ref, ref, sem, sem, sib).wait_recv()

    def left(ref, sem):
        remote(ref, ref, sem, sem, sib).wait_send()

    def turned(rr, owner):
        odd = lax.rem(rr + owner, 2)
        return x + odd * (y - x), y + odd * (x - y), odd

    def chip_at(u, v, odd):
        return (u * 4 + v) + odd * 3 * (v - u)

    column = [(dc, dz) for dz in range(4) for dc in range(2) if dc or dz]

    def cache_copy(r):
        return pltpu.make_async_copy(cache_ref.at[r], kbuf.at[r], k_sem.at[r])

    gate = pltpu.get_barrier_semaphore()
    plane = [(dx, dy) for dx in range(4) for dy in range(4) if dx or dy]
    near = [(sib, z)]
    for d in range(1, 4):
        for dc in range(2):
            near.append((2 * chip + lax.rem(core + dc, 2), lax.rem(z + d, 4)))
    for dx, dy in plane:
        near.append((2 * (lax.rem(x + dx, 4) * 4 + lax.rem(y + dy, 4)) + core, z))
    for to_ctx, to_z in near:
        pl.semaphore_signal(
            gate, inc=1, device_id={"ctx": to_ctx, "grp": to_z}, device_id_type=MESH
        )
    for i in range(REQ_DEV):
        cache_copy((lax.rem(core + i, 2)) * OWN + i // 2).start()

    def lanes_of(rr, along_y):
        return PATHS[(rr + along_y) % 2]

    for r in range(REQ_DEV):
        both = [q_ref[r, s].astype(F32) for s in range(2)]
        qf[r] = jnp.concatenate(both, axis=0)
    pl.semaphore_wait(gate, len(near))
    theirs = pl.ds((1 - core) * OWN, OWN)
    pair_q = remote(qf.at[theirs], qsib, qp_sem.at[0], qp_sem.at[1], sib)
    pair_q.start()
    rows = pl.ds(pl.multiple_of(head * 128, 128), 128)

    def column_group(cc, zz):
        return lax.rem(x + zz + 2 * cc, 4) * 2 + lax.rem(cc + y, 2)

    def cut(cc, zz):
        return proj_ref.at[:, pl.ds(pl.multiple_of(column_group(cc, zz) * COLS, 128), COLS)]

    pltpu.make_async_copy(vup_ref.at[0], vbuf.at[head], vr_sem).start()
    for dz in range(1, 4):
        remote(vup_ref.at[0], vbuf.at[head], vs_sem, vr_sem, ctx, lax.rem(z + dz, 4)).start()
    pltpu.make_async_copy(cut(core, z), wbuf.at[rows], wr_sem).start()
    for dc, dz in column:
        cc, zz = lax.rem(core + dc, 2), lax.rem(z + dz, 4)
        remote(cut(cc, zz), wbuf.at[rows], ws_sem, wr_sem, 2 * chip + cc, zz).start()

    def share_values():
        mine = vbuf.at[pl.ds(core * 4, 4)]
        arrived(mine, vr_sem)
        remote(mine, mine, vf_sem.at[0], vf_sem.at[1], sib).start()

    pair_q.wait_recv()
    for rr in range(OWN):
        r = core * OWN + rr
        mine, other = qf[r], qsib[rr]
        first = jnp.where(core == 0, mine, other)
        second = jnp.where(core == 0, other, mine)
        block = jnp.concatenate([first, second], axis=0)
        block = jnp.concatenate([block, jnp.zeros((ROWS, PADDED - WIDTH), F32)], axis=1)
        qbuf[r, x, y] = block.astype(BF16)
        for along_y in range(2):
            mine = qbuf.at[r, x, y, :, lanes_of(rr, along_y)]
            for d in range(1, 4):
                to = x * 4 + lax.rem(y + d, 4) if along_y else lax.rem(x + d, 4) * 4 + y
                remote(
                    mine, mine, q1s_sem.at[rr, along_y], q1r_sem.at[rr, along_y], 2 * to + core
                ).start()

    at = lax.broadcasted_iota(jnp.int32, (512, 512), 0)
    row = lax.broadcasted_iota(jnp.int32, (512, 512), 1)
    origin = (at % 64) // 2 * 16 + at // 256 * 8 + at % 2 * 4 + at // 64 % 4
    sort[...] = jnp.where(origin == row, 1.0, 0.0).astype(BF16)

    def spread(rr):
        r = core * OWN + rr
        for along_y in range(2):
            lanes = lanes_of(rr, along_y)
            arrived(qbuf.at[r, 0, pl.ds(0, 3), :, lanes], q1r_sem.at[rr, along_y])
            line = qbuf.at[r, x, :, :, lanes] if along_y else qbuf.at[r, :, y, :, lanes]
            for d in range(1, 4):
                to = lax.rem(x + d, 4) * 4 + y if along_y else x * 4 + lax.rem(y + d, 4)
                remote(
                    line, line, q2s_sem.at[rr, along_y], q2r_sem.at[rr, along_y], 2 * to + core
                ).start()

    def forward(rr):
        r = core * OWN + rr
        for along_y in range(2):
            lanes = lanes_of(rr, along_y)
            arrived(qbuf.at[r, pl.ds(0, 3), :, :, lanes], q2r_sem.at[rr, along_y])
        remote(qbuf.at[r], qbuf.at[r], ff_sem.at[0, r], ff_sem.at[1, r], sib).start()

    def score(r, store, part):
        odd = lax.rem(r + lax.div(r, OWN), 2)
        keys = slice(part * PART, (part + 1) * PART)
        first_pos = ctx * KEYS + part * PART
        pos = first_pos + lax.broadcasted_iota(jnp.int32, (8, PART), 1)
        draft = lax.div(lax.broadcasted_iota(jnp.int32, (8, PART), 0), 4)
        seen = (pos < len_ref[r]) | (pos == draft_ref[0, r])
        seen = seen | ((pos == draft_ref[1, r]) & (draft == 1))
        bias = jnp.where(seen, 0.0, NEG_FILL)
        queries = jnp.concatenate(
            [
                qbuf[r, k // 4 + odd * (k % 4 - k // 4), k % 4 + odd * (k // 4 - k % 4)]
                for k in range(CHIPS)
            ],
            axis=0,
        )
        scores = dot_nn(queries[:, :WIDTH], kbuf[r, :, keys])
        scores = (scores.reshape(32, 8, PART) * SCALE + bias[None]).reshape(CHIPS * ROWS, PART)
        store[:, keys] = scores
        return jnp.max(scores, axis=1, keepdims=True)

    def attend(r, store, top, ahead=None):
        total, numer, next_top = 0.0, 0.0, None
        for part in range(KEYS // PART):
            if ahead is not None:
                part_top = score(*ahead, part)
                next_top = part_top if next_top is None else jnp.maximum(next_top, part_top)
            keys = slice(part * PART, (part + 1) * PART)
            weights = jnp.exp2(store[:, keys] - top)
            total += jnp.sum(weights, axis=1, keepdims=True)
            numer += dot_nt(weights.astype(BF16), kbuf[r, :LAT, keys])
        numer = (numer * (1.0 / total)).astype(BF16)
        stat = pack_stat(top + jnp.log2(total))
        for h in range(2):
            res[r, h, :, :LAT] = numer[h * HALF:(h + 1) * HALF]
            res[r, h, :, LAT:] = stat[h * HALF:(h + 1) * HALF]
        remote(res.at[r, 1 - core], psib.at[r], ps_sem.at[r], pr_sem.at[r], sib).start()
        return next_top

    def line_to(r, i):
        owner, rr = lax.div(r, OWN), lax.rem(r, OWN)
        u, v, odd = turned(rr, owner)
        dest = 2 * chip_at(2 * core + i, v, odd) + owner
        return dest, mbuf.at[r, i], ubuf.at[rr, u], rr

    def merge(r):
        arrived(psib.at[r], pr_sem.at[r])
        a, b = res[r, core], psib[r]
        la, lb = unpack_stat(a[:, LAT:]), unpack_stat(b[:, LAT:])
        top = jnp.maximum(la, lb)
        wa, wb = jnp.exp2(la - top), jnp.exp2(lb - top)
        both = wa + wb
        inv = 1.0 / both
        merged = a[:, :LAT].astype(F32) * (wa * inv) + b[:, :LAT].astype(F32) * (wb * inv)
        stat = pack_stat(top + jnp.log2(both))
        mbuf[r, :, :, :, :LAT] = merged.astype(BF16).reshape(2, 4, ROWS, LAT)
        mbuf[r, :, :, :, LAT:] = stat.reshape(2, 4, ROWS, 128)

    def send_line(r):
        for i in range(2):
            dest, src, dst, rr = line_to(r, i)

            @pl.when(dest == ctx)
            def _():
                pltpu.make_async_copy(src, dst, ur_sem.at[rr]).start()

            @pl.when(dest != ctx)
            def _():
                remote(src, dst, us_sem.at[r, i], ur_sem.at[rr], dest).start()

    def block_to(r, i):
        owner = lax.div(r, OWN)
        u, v, odd = turned(OWN - 1, owner)
        t = lax.rem(i + 2 * v + u, 8)
        to_u, to_v = 2 * core + lax.div(t, 4), lax.rem(t, 4)
        dest = 2 * chip_at(to_u, to_v, odd) + owner
        return dest, mbuf.at[r, lax.div(t, 4), to_v], lbuf.at[chip]

    def send_blocks(r):
        def one(i, carry):
            dest, src, dst = block_to(r, i)

            @pl.when(dest == ctx)
            def _():
                pltpu.make_async_copy(src, dst, lr_sem).start()

            @pl.when(dest != ctx)
            def _():
                remote(src, dst, ls_sem.at[lax.div(r, OWN), i], lr_sem, dest).start()

            return carry

        lax.fori_loop(0, 8, one, 0)

    def joined(parts):
        lse = unpack_stat(parts[:, :, LAT:])
        top = jnp.max(lse, axis=0, keepdims=True)
        w = jnp.exp2(lse - top)
        total = jnp.sum(w, axis=0, keepdims=True)
        w = w * (1.0 / total)
        latent = jnp.sum(parts[:, :, :LAT].astype(F32) * w, axis=0)
        return latent, (top + jnp.log2(total))[0]

    def fold(rr):
        u, v, odd = turned(rr, core)
        arrived(ubuf.at[rr], ur_sem.at[rr])
        latent, lse = joined(ubuf[rr].reshape(4, 4 * ROWS, STAT))
        vout[rr, :, :, :LAT] = latent.astype(BF16).reshape(4, ROWS, LAT)
        vout[rr, :, :, LAT:] = pack_stat(lse).reshape(4, ROWS, 128)
        rbuf[rr, v] = vout[rr, v]
        for d in range(1, 4):
            to_v = lax.rem(v + d, 4)
            dest = 2 * chip_at(u, to_v, odd) + core
            remote(vout.at[rr, to_v], rbuf.at[rr, v], ns_sem.at[rr], nr_sem.at[rr], dest).start()

    def own(rr):
        return core * OWN + rr

    def other(rr):
        return (1 - core) * OWN + rr

    def came(rr):
        arrived(qbuf.at[other(rr)], ff_sem.at[1, other(rr)])
        cache_copy(other(rr)).wait()

    def merge_pair(rr):
        for owner in range(2):
            merge(owner * OWN + rr)
            send_line(owner * OWN + rr)

    spread(0)
    spread(1)
    forward(0)
    spread(2)
    cache_copy(own(0)).wait()
    top = score(own(0), store_a, 0)
    for part in range(1, KEYS // PART):
        top = jnp.maximum(top, score(own(0), store_a, part))

    def step(j, top):
        came(j)
        top = attend(own(j), store_a, top, (other(j), store_b))

        @pl.when(j > 0)
        def _():
            merge_pair(j - 1)

        @pl.when(j == 0)
        def _():
            spread(3)

        for rr in range(1, OWN):

            @pl.when(j == rr - 1)
            def _():
                forward(rr)

        cache_copy(own(j + 1)).wait()
        top = attend(other(j), store_b, top, (own(j + 1), store_a))

        @pl.when(j == OWN - 2)
        def _():
            share_values()
            fold(0)

        return top

    top = lax.fori_loop(0, OWN - 1, step, top)
    came(OWN - 1)
    top = attend(own(OWN - 1), store_a, top, (other(OWN - 1), store_b))
    merge_pair(OWN - 2)
    attend(other(OWN - 1), store_b, top)
    fold(1)
    for owner in range(2):
        merge(owner * OWN + OWN - 1)
        send_blocks(owner * OWN + OWN - 1)
    fold(OWN - 2)

    def settle():
        pair_q.wait_send()
        for rr in range(OWN):
            r = core * OWN + rr
            left(qbuf.at[r], ff_sem.at[0, r])
            for along_y in range(2):
                lanes = lanes_of(rr, along_y)
                left(qbuf.at[r, 0, pl.ds(0, 3), :, lanes], q1s_sem.at[rr, along_y])
                left(qbuf.at[r, pl.ds(0, 3), :, :, lanes], q2s_sem.at[rr, along_y])
            if rr < OWN - 1:
                left(rbuf.at[rr, pl.ds(0, 3)], ns_sem.at[rr])
        left(vbuf.at[pl.ds(0, 3)], vs_sem)
        left(vbuf.at[pl.ds(0, 4)], vf_sem.at[0])
        left(wbuf.at[pl.ds(0, 7 * 128)], ws_sem)

        def gone(r, carry):
            left(psib.at[r], ps_sem.at[r])

            @pl.when(lax.rem(r, OWN) < OWN - 1)
            def _():
                for i in range(2):
                    dest, src, dst, rr = line_to(r, i)

                    @pl.when(dest != ctx)
                    def _():
                        left(src, us_sem.at[r, i])

            @pl.when(lax.rem(r, OWN) == OWN - 1)
            def _():
                for i in range(8):
                    dest, src, dst = block_to(r, i)

                    @pl.when(dest != ctx)
                    def _():
                        left(src, ls_sem.at[lax.div(r, OWN), i])

            return carry

        lax.fori_loop(0, REQ_DEV, gone, 0)

    def finish(rr, carry):
        arrived(rbuf.at[rr, pl.ds(0, 3)], nr_sem.at[rr])
        latent, lse = joined(rbuf[rr])
        latb[rr] = latent.astype(BF16)
        return carry

    lax.fori_loop(0, OWN - 1, finish, 0)

    arrived(vbuf.at[pl.ds(4 - 4 * core, 4)], vf_sem.at[1])
    own_slot = z * 2 + core

    def head_values(start, count, which):
        latent = latb[pl.ds(start, count)].reshape(count * ROWS, LAT)
        row = lax.broadcasted_iota(jnp.int32, (count * ROWS, 128), 0)
        row_head = row // 8 % 2 * 4 + row % 4
        found = jnp.zeros((count * ROWS, 128), F32)
        for h in range(8):
            found = jnp.where(row_head == h, dot_nn(latent, vbuf[h]), found)
        part = hvall.at[own_slot, pl.ds(start, count)]
        part[...] = found.astype(BF16).reshape(count, ROWS, 128)
        for dc, dz in column:
            cc, zz = lax.rem(core + dc, 2), lax.rem(z + dz, 4)
            remote(
                part, part, hs_sem.at[which], hr_sem.at[which], 2 * chip + cc, zz
            ).start()

    head_values(0, OWN - 1, 0)
    arrived(lbuf, lr_sem)
    latb[OWN - 1] = joined(lbuf[...])[0].astype(BF16)
    head_values(OWN - 1, 1, 1)
    arrived(wbuf, wr_sem)
    settle()
    arrived(hvall.at[pl.ds(0, 7), pl.ds(0, OWN - 1)], hr_sem.at[0])
    arrived(hvall.at[pl.ds(0, 7), pl.ds(0, 1)], hr_sem.at[1])

    sorted_values = dot_nn(sort[...], hvall[...].reshape(512, 128)).astype(BF16)
    acts = jnp.concatenate([sorted_values[h * 64:(h + 1) * 64] for h in range(8)], axis=1)
    partial = dot_nn(acts, wbuf[...])
    for jj in range(4):
        piece = partial[:, jj * OUT:(jj + 1) * OUT]
        piece = jnp.concatenate([piece, jnp.zeros((64, 256 - OUT), F32)], axis=1)
        pbuf[jj] = piece.astype(BF16).reshape(4, 16, 256)

    def out_to(jj, dz):
        zz = lax.rem(z + dz, 4)
        dest = column_group(core, z) * 4 + jj
        return dest, zz, (dest == ctx) & (zz == z)

    for dz in range(4):
        for jj in range(4):
            dest, zz, here = out_to(jj, dz)

            @pl.when(here)
            def _():
                pltpu.make_async_copy(pbuf.at[jj, zz], fbuf.at[chip], fr_sem).start()

            @pl.when(jnp.logical_not(here))
            def _():
                remote(
                    pbuf.at[jj, zz], fbuf.at[chip], fs_sem.at[jj, dz], fr_sem, dest, zz
                ).start()

    arrived(fbuf, fr_sem)
    result = jnp.sum(fbuf[...].astype(F32), axis=0)[:, :OUT]
    for r in range(REQ_DEV):
        out_ref[r] = result[2 * r:2 * r + 2].astype(BF16)

    for dz in range(4):
        for jj in range(4):
            dest, zz, here = out_to(jj, dz)

            @pl.when(jnp.logical_not(here))
            def _():
                left(pbuf.at[jj, zz], fs_sem.at[jj, dz])

    left(hvall.at[pl.ds(0, 7), pl.ds(0, OWN - 1)], hs_sem.at[0])
    left(hvall.at[pl.ds(0, 7), pl.ds(0, 1)], hs_sem.at[1])


def local(query, latent_cache, context_lengths, draft_positions, value_up, out_proj):
    dma = pltpu.SemaphoreType.DMA
    vmem = pltpu.VMEM
    return pl.pallas_call(
        kernel,
        out_shape=pltpu.VMEM((REQ_DEV, 2, OUT), BF16),
        in_specs=[
            pl.BlockSpec(memory_space=pltpu.SMEM),
            pl.BlockSpec(memory_space=pltpu.SMEM),
            pl.BlockSpec(memory_space=pltpu.VMEM),
            pl.BlockSpec(memory_space=pl.ANY),
            pl.BlockSpec(memory_space=pl.ANY),
            pl.BlockSpec(memory_space=pl.ANY),
        ],
        out_specs=pl.BlockSpec(memory_space=pltpu.VMEM),
        scratch_shapes=[
            vmem((REQ_DEV, WIDTH, KEYS), BF16),
            vmem((CHIPS * ROWS, KEYS), F32),
            vmem((CHIPS * ROWS, KEYS), F32),
            vmem((REQ_DEV, 8, WIDTH), F32),
            vmem((OWN, 8, WIDTH), F32),
            vmem((REQ_DEV, 4, 4, ROWS, PADDED), BF16),
            vmem((REQ_DEV, 2, HALF, STAT), BF16),
            vmem((REQ_DEV, HALF, STAT), BF16),
            vmem((REQ_DEV, 2, 4, ROWS, STAT), BF16),
            vmem((OWN, 4, 4, ROWS, STAT), BF16),
            vmem((OWN, 4, ROWS, STAT), BF16),
            vmem((OWN, 4, ROWS, STAT), BF16),
            vmem((CHIPS, ROWS, STAT), BF16),
            vmem((OWN, ROWS, LAT), BF16),
            vmem((8 * 128, COLS), BF16),
            vmem((8, LAT, 128), BF16),
            vmem((8, OWN, ROWS, 128), BF16),
            vmem((512, 512), BF16),
            vmem((4, 4, 16, 256), BF16),
            vmem((CHIPS, 16, 256), BF16),
            dma((REQ_DEV,)), dma((2,)), dma((OWN, 2)), dma((OWN, 2)), dma((OWN, 2)), dma((OWN, 2)),
            dma((2, REQ_DEV)), dma((REQ_DEV,)), dma((REQ_DEV,)),
            dma((REQ_DEV, 2)), dma((OWN,)), dma((OWN,)), dma((OWN,)), dma((2, 8)), dma,
            dma, dma, dma, dma, dma((2,)), dma((2,)), dma((2,)), dma((4, 4)), dma,
        ],
        compiler_params=pltpu.CompilerParams(
            collective_id=0, has_side_effects=True, vmem_limit_bytes=56 * 2**20
        ),
        name="latent_decode",
    )(
        context_lengths, jnp.swapaxes(draft_positions, 0, 1), query,
        jnp.swapaxes(latent_cache, 1, 2), value_up, out_proj,
    )


def solution(mesh):
    return jax.shard_map(
        local,
        mesh=mesh,
        in_specs=(
            P("grp", None, "ctx", None),
            P("grp", "ctx", None),
            P("grp"),
            P("grp", None),
            P(("ctx", "grp"), None, None),
            P(("ctx", "grp"), None),
        ),
        out_specs=P("grp", None, "ctx"),
        check_vma=False,
    )
```

time: 62.6 us -> 56.8 us (0.907)
  Pallas kernels: 61.1 us -> 56.1 us
  local copies, waits for them, and re-layouts: 1.3 us -> 0.6 us
    pallas_call x1, Pallas kernels: 61.1 us -> 56.1 us  [local(): pl.pallas_call(kernel, out_shape=pltpu.VMEM((REQ_DEV, 2, OUT), BF16), in_...]
    unnamed x1, local copies, waits for them, and re-layouts: 1.3 us -> 0.6 us
where the time goes in v3:
time: 56.8 us; the launch traced here: 56.7 us
  Pallas kernels  56.1 us (99%)
  local copies, waits for them, and re-layouts  0.6 us (1%)
    pallas_call x1, Pallas kernels, local(): pl.pallas_call(kernel, out_shape=pltpu.VMEM((REQ_DEV, 2, OUT), BF16), in_...  56.1 us

profile of v3, /device:TPU:1, one launch (start us, length us, event | category | flops | bytes accessed | tf_op | source)
XLA Modules:
  0.0 56.7 jit_solution(1695586776869450035)
XLA Ops:
  0.0 56.1 %latent_decode.1 = bf16[8,2,224]{2,1,0:T(2,128)(2,1)S(1)} custom-call(s32[8]{0:T(128)} %len_ref.1, s32[2,8]{1,0:T(2,128)} %bitcast.3, bf16[8,2,4,576]{3,2,1,0:T(4,128)(2,1)} %q_ref.1, bf16[8,576,2048]{2,1,0:T(8,128)(2,1)} %bitcast.2, bf16[1,512,128]{2,1,0:T(8,128)(2,1)} %vup_ref.1, bf16[128,7168]{1,0:T(8,128)(2,1)} %proj_ref.1), custom_call_target="tpu_custom_call" | custom-call | tf_op jit(solution)/shard_map/latent_decode/pallas_call | solution.py:485
  56.1 0.6 %copy.8 = bf16[8,2,224]{2,1,0:T(2,128)(2,1)} copy(bf16[8,2,224]{2,1,0:T(2,128)(2,1)S(1)} %latent_decode.1) | data formatting | bytes 14336

commit v4 on v3

--- a/solution.py
+++ b/solution.py
@@ -1,3 +1,4 @@
+import functools
 import math
 
 import jax
@@ -11,6 +12,7 @@
 ROPE = 64
 NOPE = 128
 WIDTH = LAT + ROPE
+MASKED = WIDTH + 16
 PADDED = 640
 PATHS = (slice(0, 256), slice(256, PADDED))
 STAT = LAT + 128
@@ -57,8 +59,8 @@
 
 def kernel(
     len_ref, draft_ref, q_ref, cache_ref, vup_ref, proj_ref, out_ref,
-    kbuf, store_a, store_b, qf, qsib, qbuf, res, psib, mbuf, ubuf, vout, rbuf, lbuf, latb, wbuf, vbuf, hvall, sort, pbuf, fbuf,
-    k_sem, qp_sem, q1s_sem, q1r_sem, q2s_sem, q2r_sem, ff_sem, ps_sem, pr_sem,
+    kbuf, store_a, store_b, qf, qin, qbuf, res, psib, mbuf, ubuf, vout, rbuf, lbuf, latb, wbuf, vbuf, hvall, sort, pbuf, fbuf,
+    k_sem, q1s_sem, q1r_sem, q2s_sem, q2r_sem, ff_sem, ps_sem, pr_sem,
     us_sem, ur_sem, ns_sem, nr_sem, ls_sem, lr_sem, ws_sem, wr_sem, vs_sem, vr_sem, vf_sem, hs_sem, hr_sem, fs_sem, fr_sem,
 ):
     ctx = lax.axis_index("ctx")
@@ -93,33 +95,67 @@
     column = [(dc, dz) for dz in range(4) for dc in range(2) if dc or dz]
 
     def cache_copy(r):
-        return pltpu.make_async_copy(cache_ref.at[r], kbuf.at[r], k_sem.at[r])
+        return pltpu.make_async_copy(
+            cache_ref.at[r], kbuf.at[r, pl.ds(0, WIDTH)], k_sem.at[r]
+        )
 
     gate = pltpu.get_barrier_semaphore()
-    plane = [(dx, dy) for dx in range(4) for dy in range(4) if dx or dy]
     near = [(sib, z)]
     for d in range(1, 4):
         for dc in range(2):
-            near.append((2 * chip + lax.rem(core + dc, 2), lax.rem(z + d, 4)))
-    for dx, dy in plane:
-        near.append((2 * (lax.rem(x + dx, 4) * 4 + lax.rem(y + dy, 4)) + core, z))
+            cc = lax.rem(core + dc, 2)
+            near.append((2 * (lax.rem(x + d, 4) * 4 + y) + cc, z))
+            near.append((2 * (x * 4 + lax.rem(y + d, 4)) + cc, z))
+            near.append((2 * chip + cc, lax.rem(z + d, 4)))
     for to_ctx, to_z in near:
         pl.semaphore_signal(
             gate, inc=1, device_id={"ctx": to_ctx, "grp": to_z}, device_id_type=MESH
         )
-    for i in range(REQ_DEV):
-        cache_copy((lax.rem(core + i, 2)) * OWN + i // 2).start()
+    def own(rr):
+        return core * OWN + rr
+
+    def other(rr):
+        return (1 - core) * OWN + rr
+
+    order = [own(0), other(0)] + [half * OWN + rr for rr in range(1, OWN) for half in range(2)]
+    for r in order:
+        cache_copy(r).start()
+
+    pos = ctx * KEYS + lax.broadcasted_iota(jnp.int32, (16, KEYS), 1)
+    draft = lax.broadcasted_iota(jnp.int32, (16, KEYS), 0)
+    for r in range(REQ_DEV):
+        seen = (pos < len_ref[r]) | (pos == draft_ref[0, r])
+        seen = seen | ((pos == draft_ref[1, r]) & (draft == 1)) | (draft > 1)
+        kbuf[r, WIDTH:, :] = jnp.where(seen, 0.0, NEG_FILL).astype(BF16)
 
     def lanes_of(rr, along_y):
         return PATHS[(rr + along_y) % 2]
 
+    lane = lax.broadcasted_iota(jnp.int32, (8, PADDED - WIDTH), 1)
+    row_draft = lax.broadcasted_iota(jnp.int32, (8, PADDED - WIDTH), 0) // 4
+    pick = jnp.where(lane == row_draft, 1.0, 0.0)
     for r in range(REQ_DEV):
         both = [q_ref[r, s].astype(F32) for s in range(2)]
-        qf[r] = jnp.concatenate(both, axis=0)
+        block = jnp.concatenate([jnp.concatenate(both, axis=0), pick], axis=1)
+        qf[r // OWN, r % 2, r % OWN // 2] = block.astype(BF16)
+    for along_y in range(2):
+        mine = (y if along_y else x) * 2 + core
+        for odd in range(2):
+            qin[along_y, odd, mine] = qf[core, odd]
     pl.semaphore_wait(gate, len(near))
-    theirs = pl.ds((1 - core) * OWN, OWN)
-    pair_q = remote(qf.at[theirs], qsib, qp_sem.at[0], qp_sem.at[1], sib)
-    pair_q.start()
+    for odd in range(2):
+        for along_y in range(2):
+            lanes = lanes_of(odd, along_y)
+            mine = (y if along_y else x) * 2 + core
+            dst = qin.at[along_y, odd, mine, :, :, lanes]
+            for d in range(4):
+                to = x * 4 + lax.rem(y + d, 4) if along_y else lax.rem(x + d, 4) * 4 + y
+                for owner in (core, 1 - core) if d else (1 - core,):
+                    remote(
+                        qf.at[owner, odd, :, :, lanes], dst,
+                        q1s_sem.at[odd, along_y], q1r_sem.at[odd, along_y], 2 * to + owner,
+                    ).start()
+
     rows = pl.ds(pl.multiple_of(head * 128, 128), 128)
 
     def column_group(cc, zz):
@@ -141,23 +177,6 @@
         arrived(mine, vr_sem)
         remote(mine, mine, vf_sem.at[0], vf_sem.at[1], sib).start()
 
-    pair_q.wait_recv()
-    for rr in range(OWN):
-        r = core * OWN + rr
-        mine, other = qf[r], qsib[rr]
-        first = jnp.where(core == 0, mine, other)
-        second = jnp.where(core == 0, other, mine)
-        block = jnp.concatenate([first, second], axis=0)
-        block = jnp.concatenate([block, jnp.zeros((ROWS, PADDED - WIDTH), F32)], axis=1)
-        qbuf[r, x, y] = block.astype(BF16)
-        for along_y in range(2):
-            mine = qbuf.at[r, x, y, :, lanes_of(rr, along_y)]
-            for d in range(1, 4):
-                to = x * 4 + lax.rem(y + d, 4) if along_y else lax.rem(x + d, 4) * 4 + y
-                remote(
-                    mine, mine, q1s_sem.at[rr, along_y], q1r_sem.at[rr, along_y], 2 * to + core
-                ).start()
-
     at = lax.broadcasted_iota(jnp.int32, (512, 512), 0)
     row = lax.broadcasted_iota(jnp.int32, (512, 512), 1)
     origin = (at % 64) // 2 * 16 + at // 256 * 8 + at % 2 * 4 + at // 64 % 4
@@ -167,7 +186,17 @@
         r = core * OWN + rr
         for along_y in range(2):
             lanes = lanes_of(rr, along_y)
-            arrived(qbuf.at[r, 0, pl.ds(0, 3), :, lanes], q1r_sem.at[rr, along_y])
+            if rr < 2:
+                arrived(
+                    qin.at[along_y, rr, pl.ds(0, 7), :, :, lanes], q1r_sem.at[rr, along_y]
+                )
+            for k in range(4):
+                both = [qin[along_y, rr % 2, 2 * k + c, rr // 2, :, lanes] for c in range(2)]
+                block = jnp.concatenate([half.astype(F32) for half in both], axis=0)
+                if along_y:
+                    qbuf[r, x, k, :, lanes] = block.astype(BF16)
+                else:
+                    qbuf[r, k, y, :, lanes] = block.astype(BF16)
             line = qbuf.at[r, x, :, :, lanes] if along_y else qbuf.at[r, :, y, :, lanes]
             for d in range(1, 4):
                 to = lax.rem(x + d, 4) * 4 + y if along_y else x * 4 + lax.rem(y + d, 4)
@@ -185,12 +214,6 @@
     def score(r, store, part):
         odd = lax.rem(r + lax.div(r, OWN), 2)
         keys = slice(part * PART, (part + 1) * PART)
-        first_pos = ctx * KEYS + part * PART
-        pos = first_pos + lax.broadcasted_iota(jnp.int32, (8, PART), 1)
-        draft = lax.div(lax.broadcasted_iota(jnp.int32, (8, PART), 0), 4)
-        seen = (pos < len_ref[r]) | (pos == draft_ref[0, r])
-        seen = seen | ((pos == draft_ref[1, r]) & (draft == 1))
-        bias = jnp.where(seen, 0.0, NEG_FILL)
         queries = jnp.concatenate(
             [
                 qbuf[r, k // 4 + odd * (k % 4 - k // 4), k % 4 + odd * (k // 4 - k % 4)]
@@ -198,21 +221,23 @@
             ],
             axis=0,
         )
-        scores = dot_nn(queries[:, :WIDTH], kbuf[r, :, keys])
-        scores = (scores.reshape(32, 8, PART) * SCALE + bias[None]).reshape(CHIPS * ROWS, PART)
+        scores = dot_nn(queries[:, :MASKED], kbuf[r, :, keys])
         store[:, keys] = scores
         return jnp.max(scores, axis=1, keepdims=True)
 
-    def attend(r, store, top, ahead=None):
+    def attend(r, store, top, ahead=None, between=None):
         total, numer, next_top = 0.0, 0.0, None
+        top = top * SCALE
         for part in range(KEYS // PART):
             if ahead is not None:
                 part_top = score(*ahead, part)
                 next_top = part_top if next_top is None else jnp.maximum(next_top, part_top)
             keys = slice(part * PART, (part + 1) * PART)
-            weights = jnp.exp2(store[:, keys] - top)
+            weights = jnp.exp2(store[:, keys] * SCALE - top)
             total += jnp.sum(weights, axis=1, keepdims=True)
             numer += dot_nt(weights.astype(BF16), kbuf[r, :LAT, keys])
+            if part == 2 and between is not None:
+                between()
         numer = (numer * (1.0 / total)).astype(BF16)
         stat = pack_stat(top + jnp.log2(total))
         for h in range(2):
@@ -297,77 +322,67 @@
             dest = 2 * chip_at(u, to_v, odd) + core
             remote(vout.at[rr, to_v], rbuf.at[rr, v], ns_sem.at[rr], nr_sem.at[rr], dest).start()
 
-    def own(rr):
-        return core * OWN + rr
-
-    def other(rr):
-        return (1 - core) * OWN + rr
-
-    def came(rr):
-        arrived(qbuf.at[other(rr)], ff_sem.at[1, other(rr)])
-        cache_copy(other(rr)).wait()
-
-    def merge_pair(rr):
+    def came(at):
         for owner in range(2):
-            merge(owner * OWN + rr)
-            send_line(owner * OWN + rr)
+
+            @pl.when((core != owner) & (lax.div(order[at], OWN) == owner))
+            def _():
+                arrived(qbuf.at[order[at]], ff_sem.at[1, order[at]])
+
+        cache_copy(order[at]).wait()
+
+    def before(at):
+        return (order[0], order[1]) if at == 2 else (order[at - 1],) if at > 2 else ()
+
+    def merge_before(at):
+        for r in before(at):
+            merge(r)
 
     spread(0)
     spread(1)
     forward(0)
     spread(2)
-    cache_copy(own(0)).wait()
-    top = score(own(0), store_a, 0)
+    cache_copy(order[0]).wait()
+    top = score(order[0], store_a, 0)
     for part in range(1, KEYS // PART):
-        top = jnp.maximum(top, score(own(0), store_a, part))
-
-    def step(j, top):
-        came(j)
-        top = attend(own(j), store_a, top, (other(j), store_b))
-
-        @pl.when(j > 0)
-        def _():
-            merge_pair(j - 1)
-
-        @pl.when(j == 0)
-        def _():
+        top = jnp.maximum(top, score(order[0], store_a, part))
+    forward(1)
+    stores = (store_a, store_b)
+    for at in range(REQ_DEV - 1):
+        came(at + 1)
+        top = attend(
+            order[at], stores[at % 2], top, (order[at + 1], stores[1 - at % 2]),
+            functools.partial(merge_before, at),
+        )
+        for r in before(at):
+            send_line(r)
+        if at == 0:
             spread(3)
-
-        for rr in range(1, OWN):
-
-            @pl.when(j == rr - 1)
-            def _():
-                forward(rr)
-
-        cache_copy(own(j + 1)).wait()
-        top = attend(other(j), store_b, top, (own(j + 1), store_a))
-
-        @pl.when(j == OWN - 2)
-        def _():
+        if at in (1, 3):
+            forward(at // 2 + 2)
+        if at == 3:
             share_values()
+        if at == 5:
             fold(0)
-
-        return top
-
-    top = lax.fori_loop(0, OWN - 1, step, top)
-    came(OWN - 1)
-    top = attend(own(OWN - 1), store_a, top, (other(OWN - 1), store_b))
-    merge_pair(OWN - 2)
-    attend(other(OWN - 1), store_b, top)
-    fold(1)
-    for owner in range(2):
-        merge(owner * OWN + OWN - 1)
-        send_blocks(owner * OWN + OWN - 1)
+        if at == 6:
+            fold(1)
+    attend(order[REQ_DEV - 1], stores[1], top)
+    merge(order[REQ_DEV - 2])
+    send_blocks(order[REQ_DEV - 2])
+    merge(order[REQ_DEV - 1])
+    send_blocks(order[REQ_DEV - 1])
     fold(OWN - 2)
 
     def settle():
-        pair_q.wait_send()
         for rr in range(OWN):
             r = core * OWN + rr
             left(qbuf.at[r], ff_sem.at[0, r])
             for along_y in range(2):
                 lanes = lanes_of(rr, along_y)
-                left(qbuf.at[r, 0, pl.ds(0, 3), :, lanes], q1s_sem.at[rr, along_y])
+                if rr < 2:
+                    left(
+                        qin.at[along_y, rr, pl.ds(0, 7), :, :, lanes], q1s_sem.at[rr, along_y]
+                    )
                 left(qbuf.at[r, pl.ds(0, 3), :, :, lanes], q2s_sem.at[rr, along_y])
             if rr < OWN - 1:
                 left(rbuf.at[rr, pl.ds(0, 3)], ns_sem.at[rr])
@@ -495,11 +510,11 @@
         ],
         out_specs=pl.BlockSpec(memory_space=pltpu.VMEM),
         scratch_shapes=[
-            vmem((REQ_DEV, WIDTH, KEYS), BF16),
+            vmem((REQ_DEV, MASKED, KEYS), BF16),
             vmem((CHIPS * ROWS, KEYS), F32),
             vmem((CHIPS * ROWS, KEYS), F32),
-            vmem((REQ_DEV, 8, WIDTH), F32),
-            vmem((OWN, 8, WIDTH), F32),
+            vmem((2, 2, OWN // 2, 8, PADDED), BF16),
+            vmem((2, 2, 8, OWN // 2, 8, PADDED), BF16),
             vmem((REQ_DEV, 4, 4, ROWS, PADDED), BF16),
             vmem((REQ_DEV, 2, HALF, STAT), BF16),
             vmem((REQ_DEV, HALF, STAT), BF16),
@@ -515,7 +530,7 @@
             vmem((512, 512), BF16),
             vmem((4, 4, 16, 256), BF16),
             vmem((CHIPS, 16, 256), BF16),
-            dma((REQ_DEV,)), dma((2,)), dma((OWN, 2)), dma((OWN, 2)), dma((OWN, 2)), dma((OWN, 2)),
+            dma((REQ_DEV,)), dma((2, 2)), dma((2, 2)), dma((OWN, 2)), dma((OWN, 2)),
             dma((2, REQ_DEV)), dma((REQ_DEV,)), dma((REQ_DEV,)),
             dma((REQ_DEV, 2)), dma((OWN,)), dma((OWN,)), dma((OWN,)), dma((2, 8)), dma,
             dma, dma, dma, dma, dma((2,)), dma((2,)), dma((2,)), dma((4, 4)), dma,

time: 56.8 us -> 55.1 us (0.970)
  Pallas kernels: 56.1 us -> 54.3 us
    pallas_call x1, Pallas kernels: 56.1 us -> 54.3 us  [local(): pl.pallas_call(kernel, out_shape=pltpu.VMEM((REQ_DEV, 2, OUT), BF16), in_...]
where the time goes in v4:
time: 55.1 us; the launch traced here: 54.9 us
  Pallas kernels  54.3 us (99%)
  local copies, waits for them, and re-layouts  0.6 us (1%)
    pallas_call x1, Pallas kernels, local(): pl.pallas_call(kernel, out_shape=pltpu.VMEM((REQ_DEV, 2, OUT), BF16), in_...  54.3 us

profile of v4, /device:TPU:1, one launch (start us, length us, event | category | flops | bytes accessed | tf_op | source)
XLA Modules:
  0.0 54.9 jit_solution(4639993171784229031)
XLA Ops:
  0.0 54.3 %latent_decode.1 = bf16[8,2,224]{2,1,0:T(2,128)(2,1)S(1)} custom-call(s32[8]{0:T(128)} %len_ref.1, s32[2,8]{1,0:T(2,128)} %bitcast.3, bf16[8,2,4,576]{3,2,1,0:T(4,128)(2,1)} %q_ref.1, bf16[8,576,2048]{2,1,0:T(8,128)(2,1)} %bitcast.2, bf16[1,512,128]{2,1,0:T(8,128)(2,1)} %vup_ref.1, bf16[128,7168]{1,0:T(8,128)(2,1)} %proj_ref.1), custom_call_target="tpu_custom_call" | custom-call | tf_op jit(solution)/shard_map/latent_decode/pallas_call | solution.py:500
  54.3 0.6 %copy.8 = bf16[8,2,224]{2,1,0:T(2,128)(2,1)} copy(bf16[8,2,224]{2,1,0:T(2,128)(2,1)S(1)} %latent_decode.1) | data formatting | bytes 14336
